TPU v7x, 32 devices: a whole 2x2x4 slice. The times are simulated.
32 devices in a mesh: kv: 2 (over x), qh: 2 (over y), seq: 8 (over z, core).
Axes of the slice: x: 2, y: 2, z: 4, core: 2. Of those that a mesh axis runs over, the one named last changes fastest.
Arguments:
- tokens: bfloat16 [8, 1024, 1536], P(('kv', 'qh'), 'seq'), may hold values from -6 to 6
- attn_gain: bfloat16 [1536], replicated, may hold values from 0.5 to 1.5
- query_weight: bfloat16 [1536, 1536], P(None, ('kv', 'qh')), may hold values from -0.15625 to 0.15625
- query_bias: bfloat16 [1536], P(('kv', 'qh')), may hold values from -3 to 3
- key_matrix: bfloat16 [1536, 256], P(None, 'kv'), may hold values from -0.15625 to 0.15625
- key_offset_bias: bfloat16 [256], P('kv'), may hold values from -3 to 3
- value_matrix: bfloat16 [1536, 256], P(None, 'kv'), may hold values from -0.15625 to 0.15625
- value_offset_bias: bfloat16 [256], P('kv'), may hold values from -0.29882812 to 0.29882812
- out_weight: bfloat16 [1536, 1536], P(('kv', 'qh')), may hold values from -1.25 to 1.25
- mlp_gain: bfloat16 [1536], replicated, may hold values from 0.5 to 1.5
- gate_weight: bfloat16 [1536, 8960], P(None, ('kv', 'qh')), may hold values from -0.15625 to 0.15625
- up_weight: bfloat16 [1536, 8960], P(None, ('kv', 'qh')), may hold values from -0.15625 to 0.15625
- down_weight: bfloat16 [8960, 1536], P(('kv', 'qh')), may hold values from -0.0625 to 0.0625
- segment_ids: int32 [8, 1024], replicated, may hold values from 0 to 4, as said below
- position_ids: int32 [8, 1024], P(None, 'seq'), may hold values from 0 to 1023, as said below
- cotangent: bfloat16 [8, 1024, 1536], P(('kv', 'qh'), 'seq'), may hold values from -6 to 6
Outputs:
- output: bfloat16 [8, 1024, 1536], P(('kv', 'qh'), 'seq')
- tokens_grad: float32 [8, 1024, 1536], P(('kv', 'qh'), 'seq')
- attn_gain_grad: float32 [1536], replicated
- query_weight_grad: float32 [1536, 1536], P('seq', ('kv', 'qh'))
- query_bias_grad: float32 [1536], replicated
- key_weight_grad: float32 [1536, 256], replicated
- key_bias_grad: float32 [256], replicated
- value_weight_grad: float32 [1536, 256], replicated
- value_bias_grad: float32 [256], replicated
- out_weight_grad: float32 [1536, 1536], P(('kv', 'qh'), 'seq')
- mlp_gain_grad: float32 [1536], replicated
- gate_weight_grad: float32 [1536, 8960], P('seq', ('kv', 'qh'))
- up_weight_grad: float32 [1536, 8960], P('seq', ('kv', 'qh'))
- down_weight_grad: float32 [8960, 1536], P(('kv', 'qh'), 'seq')
Inputs may be any that keep to these rules, and one draw needn't show every extreme that they name: `segment_ids`: along each row the ids start at 0 and never fall. `position_ids`: count from 0 at the first token of each run of equal segment ids and rise by one within it.
All inputs are finite; a program needn't handle non-finite values.
Results may differ from a plain program's by a relative error of at most 0.035.
Values may be sent and summed in bfloat16 or wider, within the bound.
A program may use at most 320 MiB of HBM per device.

v0:
```python
import functools
import types
import jax
import jax.numpy as jnp
from jax import lax
from jax.experimental import pallas as pl
from jax.experimental.pallas import tpu as pltpu
from jax.sharding import PartitionSpec as P

epsilon = 1e-06
rope_base = 1000000.0
MESH = pl.DeviceIdType.MESH
ANY = pl.BlockSpec(memory_space=pl.ANY)
VMEM = pl.BlockSpec(memory_space=pltpu.VMEM)
bf16 = jnp.bfloat16
f32 = jnp.float32


class Place:
    def __init__(self, seq_size):
        k, q, s = lax.axis_index("kv"), lax.axis_index("qh"), lax.axis_index("seq")
        self.kv, self.qh, self.seq = k, q, s
        self.chip, self.core = s // 2, lax.rem(s, 2)
        self.chips = seq_size // 2
        self.across_x = (1 - k, q, s)
        self.across_y = (k, 1 - q, s)
        self.diagonal = (1 - k, 1 - q, s)
        self.sibling = (k, q, s + 1 - 2 * self.core)
        self.above = (k, q, s + 2)
        self.below = (k, q, s - 2)
        self.has_above = self.chip < self.chips - 1
        self.has_below = self.chip > 0


class Wires:
    def __init__(self, send, recv, local):
        self.send, self.recv, self.local = send, recv, local
        self.count, self.local_count = 0, 2

    def reserve(self, count):
        self.count += count
        return self.count - count

    def remote(self, src, dst, device):
        return self.at(self.reserve(1), src, dst, device)

    def at(self, i, src, dst, device):
        return pltpu.make_async_remote_copy(
            src_ref=src,
            dst_ref=dst,
            send_sem=self.send.at[i],
            recv_sem=self.recv.at[i],
            device_id=device,
            device_id_type=MESH,
        )

    def copy(self, src, dst):
        i = self.local_count
        self.local_count += 1
        return pltpu.make_async_copy(src, dst, self.local.at[i])

    def fetch(self, sources, targets):
        copies = [pltpu.make_async_copy(a, b, self.local.at[i]) for i, (a, b) in enumerate(zip(sources, targets))]
        for copy in copies:
            copy.start()
        for copy in copies:
            copy.wait()


def greet(devices, conditional):
    barrier = pltpu.get_barrier_semaphore()
    for device in devices:
        pl.semaphore_signal(barrier, inc=1, device_id=device, device_id_type=MESH)
    for present, device in conditional:

        @pl.when(present)
        def _(device=device):
            pl.semaphore_signal(barrier, inc=1, device_id=device, device_id_type=MESH)

    return barrier


def dot(a, b, dims=((1,), (0,))):
    return lax.dot_general(a, b, (dims, ((), ())), preferred_element_type=f32)


def turn(v, cosine, sine):
    return v * cosine + pltpu.roll(v, v.shape[-1] // 2, v.ndim - 1) * sine


class WeightGather:
    def __init__(self, place, wires, own, gathered):
        rows = own.shape[0]
        half, quarter = rows // 2, rows // 4
        self.place, self.gathered = place, gathered
        base = place.core * half
        mine = pl.ds(pl.multiple_of(base, half), half)
        first = pl.ds(pl.multiple_of(base, quarter), quarter)
        second = pl.ds(pl.multiple_of(base + quarter, quarter), quarter)
        g = gathered
        self.x = wires.remote(own.at[mine], g.at[0, mine], place.across_x)
        self.y = wires.remote(own.at[mine], g.at[1, mine], place.across_y)
        self.dx = wires.remote(g.at[1, first], g.at[2, first], place.across_x)
        self.dy = wires.remote(g.at[0, second], g.at[2, second], place.across_y)
        self.share = [
            wires.remote(g.at[0, mine], g.at[0, mine], place.sibling),
            wires.remote(g.at[1, mine], g.at[1, mine], place.sibling),
            wires.remote(g.at[2, first], g.at[2, first], place.sibling),
            wires.remote(g.at[2, second], g.at[2, second], place.sibling),
        ]

    def begin(self):
        self.x.start()
        self.y.start()

    def got_x(self):
        self.x.wait_recv()
        self.dy.start()
        self.share[0].start()

    def got_y(self):
        self.y.wait_recv()
        self.dx.start()
        self.share[1].start()

    def got_diagonal(self):
        self.dx.wait_recv()
        self.share[2].start()
        self.dy.wait_recv()
        self.share[3].start()

    def complete(self, block):
        for i in ((0,), (1,), (2, 3))[block]:
            self.share[i].wait_recv()

    def drain(self):
        for copy in [self.x, self.y, self.dx, self.dy] + self.share:
            copy.wait_send()


class TokenGather:
    def __init__(self, place, wires, own, gathered):
        half = own.shape[0] // 2
        g = gathered
        self.x = wires.remote(own, g.at[1], place.across_x)
        self.y = wires.remote(own, g.at[2], place.across_y)
        self.dx = wires.remote(g.at[2, pl.ds(0, half)], g.at[3, pl.ds(0, half)], place.across_x)
        self.dy = wires.remote(g.at[1, pl.ds(half, half)], g.at[3, pl.ds(half, half)], place.across_y)

    def begin(self):
        self.x.start()
        self.y.start()

    def relay(self):
        self.y.wait_recv()
        self.dx.start()
        self.x.wait_recv()
        self.dy.start()

    def finish(self):
        self.dx.wait_recv()
        self.dy.wait_recv()
        for copy in (self.x, self.y, self.dx, self.dy):
            copy.wait_send()


def as_column(row):
    count = row.shape[1]
    here = lax.broadcasted_iota(jnp.int32, (count, count), 0) == lax.broadcasted_iota(jnp.int32, (count, count), 1)
    return jnp.sum(jnp.where(here, jnp.broadcast_to(row, (count, count)), jnp.zeros_like(row)), axis=1, keepdims=True)


def row_of(array, index):
    here = lax.broadcasted_iota(jnp.int32, array.shape, 0) == index
    return jnp.sum(jnp.where(here, array, jnp.zeros_like(array)), axis=0, keepdims=True)


def front_kernel(
    seq_size,
    tok_ref, cot_ref, pack_ref, wq_ref, wk_ref, wv_ref, wo_ref, cos_ref, sin_ref, seg_ref, wg_ref, wu_ref, wd_ref,
    wqg_ref, wog_ref, wkvg_ref, x2g_ref, cotg_ref, hidden_ref, n1_ref, q_ref, kv_ref, p_ref, ctx_ref, act_ref, gg_ref, gu_ref,
    packs, kv_v, ctx_v, hidden_v, x2_v, cot_v, wo_v, wog_v, wqg_v, p_sems, send, recv, local,
):
    place = Place(seq_size)
    wires = Wires(send, recv, local)
    chips = place.chips
    tok, width = tok_ref.shape
    span = tok // 2
    keys = kv_v.shape[2]
    hd = cos_ref.shape[1]
    qw = wq_ref.shape[1]
    heads = qw // hd
    ff = wg_ref.shape[0]

    kv_v[...] = jnp.zeros_like(kv_v)
    barrier = greet(
        [place.across_x, place.across_y, place.diagonal, place.sibling], [(place.has_below, place.below)]
    )
    pl.semaphore_wait(barrier, 4 + jnp.where(place.has_above, 1, 0))

    half = width // 2
    mine = pl.ds(pl.multiple_of(place.core * half, half), half)
    kvx = [
        wires.remote(wk_ref.at[mine], wkvg_ref.at[mine, pl.ds(0, hd)], place.across_x),
        wires.remote(wv_ref.at[mine], wkvg_ref.at[mine, pl.ds(hd, hd)], place.across_x),
    ]
    kvs = wires.remote(wkvg_ref.at[mine], wkvg_ref.at[mine], place.sibling)
    packed = [
        wires.remote(pack_ref, packs.at[i], device)
        for i, device in enumerate((place.across_x, place.across_y, place.diagonal))
    ]
    gq = WeightGather(place, wires, wq_ref, wqg_v)
    go = WeightGather(place, wires, wo_ref, wog_v)
    for copy in kvx + packed:
        copy.start()
    gq.begin()

    def block(seq_index):
        return kv_v.at[:, :, pl.ds(pl.multiple_of(seq_index * span, span), span), :]

    ups = []
    shares = []
    for j in range(chips):
        ups.append(wires.remote(block(place.seq - 2 * j), block(place.seq - 2 * j), place.above) if j < chips - 1 else None)
        shares.append(wires.remote(block(place.seq - 2 * j), block(place.seq - 2 * j), place.sibling))

    def chain(j):
        @pl.when(place.chip >= j)
        def _():
            if j > 0:
                ups[j - 1].wait_recv()
            shares[j].start()
            if j < chips - 1:

                @pl.when(place.has_above)
                def _():
                    ups[j].start()

    gather_two = TokenGather(place, wires, x2_v.at[0], x2_v)
    gather_cot = TokenGather(place, wires, cot_ref, cot_v)
    load_o = wires.copy(wo_ref, wo_v)
    load_cot = wires.copy(cot_ref, cot_v.at[0])
    save_wq = wires.copy(wqg_v, wqg_ref)
    save_wo = wires.copy(wog_v, wog_ref)
    save_two = wires.copy(x2_v, x2g_ref)
    save_cot = wires.copy(cot_v, cotg_ref)
    load_cot.start()
    save_kv = wires.copy(kv_v, kv_ref)
    save_ctx = wires.copy(ctx_v, ctx_ref)
    save_hidden = wires.copy(hidden_v, hidden_ref)
    load_o.start()
    first_row = (2 * place.kv + place.qh) * 2

    def attention(wkv_v, wq_v, n1_v, q_v, mask_v, p_v):
        load_kv = [wires.copy(wk_ref, wkv_v.at[0, :, pl.ds(0, hd)]), wires.copy(wv_ref, wkv_v.at[0, :, pl.ds(hd, hd)])]
        load_q = wires.copy(wq_ref, wq_v)
        for copy in load_kv + [load_q]:
            copy.start()

        tokens = tok_ref[...].astype(f32)
        factor = lax.rsqrt(jnp.mean(tokens * tokens, axis=-1, keepdims=True) + epsilon)
        n1_v[...] = (tokens * factor * pack_ref[0:1, :]).astype(bf16)
        save_n1 = wires.copy(n1_v, n1_ref)
        save_n1.start()

        here = pl.ds(pl.multiple_of(place.seq * span, span), span)

        def biases_of(i):
            row = pack_ref[2:3, :] if i == 0 else packs[i - 1, 2:3, :]
            return row[:, :qw], row[:, qw : qw + hd], row[:, qw + hd : qw + 2 * hd]

        def project_kv(head):
            _, kbias, vbias = biases_of(head)
            both = dot(n1_v[...], wkv_v[head])
            rotated = turn(both[:, :hd] + kbias, cos_ref[...], sin_ref[...]).astype(bf16)
            kv_v[2 * head, :, here, :] = rotated.reshape(2, span, hd)
            kv_v[2 * head + 1, :, here, :] = (both[:, hd:] + vbias).astype(bf16).reshape(2, span, hd)

        for copy in load_kv:
            copy.wait()
        project_kv(0)
        for copy in kvx:
            copy.wait_recv()
        kvs.start()
        kvs.wait_recv()
        load_kvx = wires.copy(wkvg_ref, wkv_v.at[1])
        load_kvx.start()
        for copy in packed:
            copy.wait_recv()
        load_kvx.wait()
        project_kv(1)
        chain(0)
        load_q.wait()

        def project_q(i):
            weight = wq_v[...] if i == 0 else wqg_v[i - 1]
            lin = dot(n1_v[...], weight) + biases_of(i)[0]
            for h in range(heads):
                part = turn(lin[:, h * hd : (h + 1) * hd], cos_ref[...], sin_ref[...]).astype(bf16)
                q_v[i, 0, h] = part[:span]
                q_v[i, 1, h] = part[span:]

        project_q(0)
        gq.got_y()
        go.y.start()
        gq.got_x()
        go.x.start()
        for j in range(1, (chips + 1) // 2):
            chain(j)
        for i in (1, 2):
            gq.complete(i - 1)
            project_q(i)
        gq.got_diagonal()
        for j in range((chips + 1) // 2, chips):
            chain(j)
        gq.complete(2)
        save_wq.start()
        project_q(3)
        save_q = wires.copy(q_v, q_ref)
        save_q.start()
        for j in range(chips):

            @pl.when(place.chip >= j)
            def _(j=j):
                shares[j].wait_recv()

        save_kv.start()
        scaling = hd ** (-0.5)
        key_order = lax.broadcasted_iota(jnp.int32, (span, keys), 1)
        query_order = lax.broadcasted_iota(jnp.int32, (span, keys), 0) + place.seq * span

        def save_p(r, i):
            slot = lax.rem(i, 2)
            return pltpu.make_async_copy(p_v.at[slot], p_ref.at[r, i], p_sems.at[slot])

        def attend(r):
            key_segs = row_of(seg_ref[...], first_row + r)
            query_segs = as_column(row_of(seg_ref[:, here], first_row + r))
            allowed = (key_order <= query_order) & (query_segs == key_segs)
            mask_v[...] = jnp.where(allowed, 0.0, -1e30)

            def unit(i, carry):
                kvh = lax.rem(i, 2)
                slot = lax.rem(i, 2)
                queries = q_v[i, r].reshape(heads * span, hd)
                scores = dot(queries, kv_v[2 * kvh, r], ((1,), (1,))) * scaling
                scores = scores.reshape(heads, span, keys) + mask_v[...][None]
                row_max = jnp.max(scores, axis=-1, keepdims=True)
                exponent = jnp.exp(scores - row_max)
                total = jnp.sum(exponent, axis=-1, keepdims=True)
                probs = (exponent * (1.0 / total)).astype(bf16)

                @pl.when(i >= 2)
                def _():
                    save_p(r, i - 2).wait()

                p_v[slot] = probs.reshape(heads * span, keys)
                save_p(r, i).start()
                context = dot(p_v[slot], kv_v[2 * kvh + 1, r]).astype(bf16)
                for h in range(heads):
                    ctx_v[i, r * span : (r + 1) * span, h * hd : (h + 1) * hd] = context[h * span : (h + 1) * span]
                return carry

            lax.fori_loop(0, 4, unit, 0)
            for i in (2, 3):
                pltpu.make_async_copy(p_v.at[i % 2], p_ref.at[r, i], p_sems.at[i % 2]).wait()

        go.got_y()
        attend(0)
        go.got_x()
        gather_cot.begin()
        attend(1)
        go.got_diagonal()
        save_n1.wait()
        save_q.wait()

    pl.run_scoped(
        attention,
        pltpu.VMEM((2, width, 2 * hd), bf16),
        pltpu.VMEM((width, qw), bf16),
        pltpu.VMEM((tok, width), bf16),
        pltpu.VMEM((4, 2, heads, span, hd), bf16),
        pltpu.VMEM((span, keys), f32),
        pltpu.VMEM((2, heads * span, keys), bf16),
    )
    save_ctx.start()

    def feed_forward(wg, wu, wd, grads, stage):
        loads = [wires.copy(wd_ref, wd), wires.copy(wg_ref, wg), wires.copy(wu_ref, wu)]
        for copy in loads:
            copy.start()
        load_o.wait()
        hidden_v[...] = tok_ref[...].astype(f32) + dot(ctx_v[0], wo_v[...])
        for i in (1, 2, 3):
            go.complete(i - 1)
            hidden_v[...] += dot(ctx_v[i], wog_v[i - 1])
        hidden = hidden_v[...]
        factor = lax.rsqrt(jnp.mean(hidden * hidden, axis=-1, keepdims=True) + epsilon)
        x2_v[0] = (hidden * factor * pack_ref[1:2, :]).astype(bf16)
        gather_two.begin()
        save_hidden.start()
        save_wo.start()
        whole = ff // 256
        saves = []

        def each_tile(tile):
            def some(i, carry):
                tile(pl.ds(pl.multiple_of(i * 256, 256), 256))
                return carry

            lax.fori_loop(0, whole, some, 0)
            if ff % 256:
                tile(pl.ds(whole * 256, ff % 256))

        def gradients(b):
            def tile(units):
                grads[b, :, units] = dot(cot_v[b], wd[units, :], ((1,), (1,))).astype(bf16)

            each_tile(tile)

        def activations(b):
            slot = b % 2
            if b >= 2:
                for copy in saves[b - 2]:
                    copy.wait()

            def tile(units):
                gate = dot(x2_v[b], wg[units, :], ((1,), (1,)))
                up = dot(x2_v[b], wu[units, :], ((1,), (1,)))
                grad = grads[b, :, units].astype(f32)
                sig = jax.nn.sigmoid(gate)
                silu = gate * sig
                stage[slot, 0, :, units] = (silu * up).astype(bf16)
                stage[slot, 1, :, units] = (grad * up * sig * (1.0 + gate * (1.0 - sig))).astype(bf16)
                stage[slot, 2, :, units] = (grad * silu).astype(bf16)

            each_tile(tile)
            rows = pl.ds(b * tok, tok)
            copies = [wires.copy(stage.at[slot, i], ref.at[rows]) for i, ref in enumerate((act_ref, gg_ref, gu_ref))]
            for copy in copies:
                copy.start()
            saves.append(copies)

        loads[0].wait()
        load_cot.wait()
        gradients(0)
        gather_cot.relay()
        gradients(1)
        loads[1].wait()
        loads[2].wait()
        activations(0)
        gradients(2)
        gather_two.relay()
        activations(1)
        gather_cot.finish()
        save_cot.start()
        gradients(3)
        activations(2)
        gather_two.finish()
        save_two.start()
        activations(3)
        for copies in saves[2:]:
            for copy in copies:
                copy.wait()

    pl.run_scoped(
        feed_forward,
        pltpu.VMEM((ff, width), bf16),
        pltpu.VMEM((ff, width), bf16),
        pltpu.VMEM((ff, width), bf16),
        pltpu.VMEM((4, tok, ff), bf16),
        pltpu.VMEM((2, 3, tok, ff), bf16),
    )

    for copy in [save_kv, save_ctx, save_hidden, save_wq, save_wo, save_two, save_cot]:
        copy.wait()
    for copy in kvx + [kvs] + packed:
        copy.wait_send()
    gq.drain()
    go.drain()
    for j in range(chips):

        @pl.when(place.chip >= j)
        def _(j=j):
            shares[j].wait_send()
            if j < chips - 1:

                @pl.when(place.has_above)
                def _():
                    ups[j].wait_send()


def front(seq_size, tok, cot, pack, wq, wk, wv, wo, cosine, sine, segs, wg, wu, wd):
    tokens, width = tok.shape
    span = tokens // 2
    qw, hd = wq.shape[1], cosine.shape[1]
    heads = qw // hd
    keys = segs.shape[1]
    chips = seq_size // 2
    ff = wg.shape[0]
    shape = jax.ShapeDtypeStruct
    outs = (
        shape((3, width, qw), bf16),
        shape((3, qw, width), bf16),
        shape((width, 2 * hd), bf16),
        shape((4, tokens, width), bf16),
        shape((4, tokens, width), bf16),
        shape((tokens, width), f32),
        shape((tokens, width), bf16),
        shape((4, 2, heads, span, hd), bf16),
        shape((4, 2, keys, hd), bf16),
        shape((2, 4, heads * span, keys), bf16),
        shape((4, tokens, qw), bf16),
        shape((4 * tokens, ff), bf16),
        shape((4 * tokens, ff), bf16),
        shape((4 * tokens, ff), bf16),
    )
    remotes = 6 + 8 + 8 + 2 * chips + 8
    scratch = [
        pltpu.VMEM((3,) + pack.shape, f32),
        pltpu.VMEM((4, 2, keys, hd), bf16),
        pltpu.VMEM((4, tokens, qw), bf16),
        pltpu.VMEM((tokens, width), f32),
        pltpu.VMEM((4, tokens, width), bf16),
        pltpu.VMEM((4, tokens, width), bf16),
        pltpu.VMEM((qw, width), bf16),
        pltpu.VMEM((3, qw, width), bf16),
        pltpu.VMEM((3, width, qw), bf16),
        pltpu.SemaphoreType.DMA((2,)),
        pltpu.SemaphoreType.DMA((remotes,)),
        pltpu.SemaphoreType.DMA((remotes,)),
        pltpu.SemaphoreType.DMA((40,)),
    ]
    return pl.pallas_call(
        functools.partial(front_kernel, seq_size),
        out_shape=outs,
        in_specs=[VMEM, ANY, VMEM, ANY, ANY, ANY, ANY, VMEM, VMEM, VMEM, ANY, ANY, ANY],
        out_specs=tuple([ANY] * len(outs)),
        scratch_shapes=scratch,
        name="attention_front",
        compiler_params=pltpu.CompilerParams(
            collective_id=0, has_side_effects=True, vmem_limit_bytes=62 * 2**20
        ),
    )(tok, cot, pack, wq, wk, wv, wo, cosine, sine, segs, wg, wu, wd)


def add_rows(total, extra, step=32):
    rows = total.shape[0]
    step = step if rows % step == 0 else 16

    def body(i, carry):
        here = pl.ds(pl.multiple_of(i * step, step), step)
        total[here, :] = total[here, :] + extra[here, :]
        return carry

    lax.fori_loop(0, rows // step, body, 0)


class LineSum:
    def __init__(self, place, wires, totals, landing, room):
        self.place, self.wires, self.totals, self.landing, self.room = place, wires, totals, landing, room
        self.last = place.chips - 1
        self.first = wires.reserve(2 * self.last)

    def up(self, t):
        d = self.last - t
        return self.wires.at(self.first + t, self.totals.at[d], self.landing.at[0, d], self.place.above)

    def down(self, t):
        return self.wires.at(
            self.first + self.last + t, self.totals.at[t], self.landing.at[1, t], self.place.below
        )

    def take(self, way, d):
        self.wires.fetch((self.landing.at[way, d],), (self.room,))
        add_rows(self.totals.at[d], self.room)

    def send(self, w):
        z, last = self.place.chip, self.last

        @pl.when(z == 0)
        def _():
            self.up(w).start()

        @pl.when(z == last)
        def _():
            self.down(w).start()

    def forward(self, w):
        z, last = self.place.chip, self.last
        t = w - z

        @pl.when((z > 0) & (t >= 0))
        def _():
            self.up(t).wait_recv()
            self.take(0, last - t)
            self.up(t).start()

        u = w - (last - z)

        @pl.when((z < last) & (u >= 0))
        def _():
            self.down(u).wait_recv()
            self.take(1, u)
            self.down(u).start()

    def finish(self):
        z, last = self.place.chip, self.last

        @pl.when(z > 0)
        def _():
            self.up(last - z).wait_recv()
            self.take(0, z)

        @pl.when(z < last)
        def _():
            self.down(z).wait_recv()
            self.take(1, z)

        for t in range(last):

            @pl.when(t < last - z)
            def _(t=t):
                self.up(t).wait_send()

            @pl.when(t < z)
            def _(t=t):
                self.down(t).wait_send()


class LineSumDown:
    def __init__(self, place, wires, totals, landing, room):
        self.place, self.wires, self.totals, self.landing, self.room = place, wires, totals, landing, room
        self.last = place.chips - 1
        self.first = wires.reserve(self.last)

    def down(self, t):
        return self.wires.at(self.first + t, self.totals(t), self.landing.at[t], self.place.below)

    def take(self, d):
        self.wires.fetch((self.landing.at[d],), (self.room,))
        add_rows(self.totals(d), self.room)

    def send(self, w):
        @pl.when(self.place.chip == self.last)
        def _():
            self.down(w).start()

    def forward(self, w):
        z, last = self.place.chip, self.last
        u = w - (last - z)

        @pl.when((z < last) & (u >= 0))
        def _():
            self.down(u).wait_recv()
            self.take(u)
            self.down(u).start()

    def finish(self):
        z, last = self.place.chip, self.last

        @pl.when(z < last)
        def _():
            self.down(z).wait_recv()
            self.take(z)

        for t in range(last):

            @pl.when(t < z)
            def _(t=t):
                self.down(t).wait_send()


class Spread:
    def __init__(self, place, wires, source, target):
        self.place, self.wires, self.source, self.target = place, wires, source, target
        self.first = wires.reserve(place.chips)

    def copy(self, chip_from, chip_to):
        place, wires = self.place, self.wires
        return pltpu.make_async_remote_copy(
            src_ref=self.source(chip_to),
            dst_ref=self.target(chip_from),
            send_sem=wires.send.at[self.first + chip_to],
            recv_sem=wires.recv.at[self.first + chip_from],
            device_id=(place.kv, place.qh, 2 * chip_to + place.core),
            device_id_type=MESH,
        )

    def others(self, action):
        for d in range(self.place.chips):

            @pl.when(self.place.chip != d)
            def _(d=d):
                action(d)

    def send(self):
        self.others(lambda d: self.copy(self.place.chip, d).start())

    def receive(self, then=None):
        def take(d):
            self.copy(d, d).wait_recv()
            if then is not None:
                then(d)

        self.others(take)

    def drain(self):
        self.others(lambda d: self.copy(self.place.chip, d).wait_send())


class PlaneSum:
    def __init__(self, place, wires, parts, from_x, from_y, land_x, land_y, rooms=None):
        self.wires, self.rooms = wires, rooms
        rows = parts.shape[0] // 4
        half = rows // 2
        self.rows, self.half, self.parts = rows, half, parts
        self.from_x, self.from_y, self.land_x, self.land_y = from_x, from_y, land_x, land_y
        lo, hi = pl.ds(0, half), pl.ds(half, half)

        def block(i, upper):
            return parts.at[pl.ds(i * rows + (half if upper else 0), half)]

        x, y = place.across_x, place.across_y
        self.first = [
            wires.remote(block(3, 0), from_x, x),
            wires.remote(block(3, 1), from_y, y),
            wires.remote(block(1, 0), land_x.at[lo], x),
            wires.remote(block(2, 1), land_y.at[hi], y),
        ]
        self.second = [
            wires.remote(block(1, 1), land_x.at[hi], x),
            wires.remote(block(2, 0), land_y.at[lo], y),
        ]
        self.block = block

    def begin(self):
        for copy in self.first:
            copy.start()

    def middle(self):
        near = (self.from_x, self.from_y)
        self.first[0].wait_recv()
        self.first[1].wait_recv()
        if self.rooms is not None:
            landed, near = near, [room.at[pl.ds(0, self.half)] for room in self.rooms]
            self.wires.fetch(landed, near)
        add_rows(self.block(2, 0), near[0])
        self.second[1].start()
        add_rows(self.block(1, 1), near[1])
        self.second[0].start()

    def end(self):
        for copy in self.first[2:] + self.second:
            copy.wait_recv()
        for copy in self.first + self.second:
            copy.wait_send()
        if self.rooms is not None:
            self.wires.fetch((self.land_x, self.land_y), self.rooms)
            self.land_x, self.land_y = self.rooms

    def value(self, here):
        return (
            self.parts[here, :].astype(f32) + self.land_x[here, :].astype(f32) + self.land_y[here, :].astype(f32)
        )


def back_kernel(seq_size, names, *refs):
    r = types.SimpleNamespace(**dict(zip(names, refs)))
    place = Place(seq_size)
    wires = Wires(r.send, r.recv, r.local)
    chips, z, c = place.chips, place.chip, place.core
    last = chips - 1
    ff, width = r.wg.shape
    rb = width // (2 * chips)
    tokens = r.tok.shape[0]
    span = tokens // 2
    hd = r.cos.shape[1]
    qw = r.wq.shape[1]
    heads = qw // hd
    barrier = greet(
        [place.sibling, place.across_x, place.across_y],
        [(z != d, (place.kv, place.qh, 2 * d + c)) for d in range(chips)],
    )
    pl.semaphore_wait(barrier, 3 + last)

    ffsum, ffroom = r.ffsum, r.ffroom
    lines = [LineSum(place, wires, ffsum.at[m], r.ffland.at[m], ffroom) for m in range(3)]
    plane_two = PlaneSum(place, wires, r.part_two, r.two_fx, r.two_fy, r.two_lx, r.two_ly)
    waits = {}

    def ff_phase(rows_in, act, gg, gu, full, wbuf):
        loads = {}
        for name, dst in (("cotg", rows_in), ("act", act), ("gg", gg), ("gu", gu), ("x2g", rows_in)):
            loads[name] = wires.copy(getattr(r, name), dst)
        tile = 512
        tiles = width // tile
        for name in ("cotg", "act"):
            loads[name].start()
        gate_streams, down_streams = [], []
        for n in range(tiles):
            cols = pl.ds(n * tile, tile)
            gate_streams.append(
                [
                    wires.copy(r.wg.at[:, cols], wbuf.at[n % 2, 0]),
                    wires.copy(r.wu.at[:, cols], wbuf.at[n % 2, 1]),
                ]
            )
            down_streams.append(wires.copy(r.wd.at[:, cols], wbuf.at[n % 2, 0]))

        block = 384
        blocks = width // block
        per = block // (2 * rb)
        order = []
        for i in range((blocks + 1) // 2):
            order += [blocks - 1 - i] + ([i] if i != blocks - 1 - i else [])
        pending = [[] for _ in range(3)]

        def weight_grad(m, left, right, then={}):
            for n, i in enumerate(order):
                before = pending[m][n - 2] if n > 1 else (pending[m - 1][n - 2] if m > 0 else None)
                if before is not None:
                    before[0].wait_send()
                for lo in range(0, ff, 512):
                    hi = min(ff, lo + 512)
                    value = dot(left[:, i * block : (i + 1) * block], right[:, lo:hi], ((0,), (0,)))
                    full[n % 2, :, :, :, lo:hi] = value.astype(bf16).reshape(per, 2, rb, hi - lo)
                chunk = pl.ds(i * per, per)
                copy = wires.remote(full.at[n % 2, :, 1 - c], ffsum.at[m, chunk], place.sibling)
                copy.start()
                pending[m].append((copy, i))
                if n > 0:
                    settle(m, n - 1)
                if n in then:
                    then[n]()
            settle(m, len(order) - 1)

        def settle(m, n):
            copy, i = pending[m][n]
            copy.wait_recv()
            for j in range(per):
                add_rows(ffsum.at[m, i * per + j], full.at[n % 2, j, c])

        loads["cotg"].wait()
        loads["act"].wait()
        for copy in [loads["gg"], loads["gu"]] + gate_streams[0]:
            copy.start()
        weight_grad(0, rows_in, act, {2: lambda: lines[0].send(0)})
        loads["x2g"].start()
        for w in range(1, last):
            lines[0].send(w)

        loads["gg"].wait()
        loads["gu"].wait()
        for n in range(tiles):
            for copy in gate_streams[n]:
                copy.wait()
            if n + 1 < tiles:
                for copy in gate_streams[n + 1]:
                    copy.start()
            for lo in range(0, tile, 256):
                value = dot(gg[...], wbuf[n % 2, 0, :, lo : lo + 256])
                value = value + dot(gu[...], wbuf[n % 2, 1, :, lo : lo + 256])
                r.part_two[:, n * tile + lo : n * tile + lo + 256] = value.astype(bf16)
        down_streams[0].start()
        plane_two.begin()
        loads["x2g"].wait()
        if last > 1:
            lines[0].forward(1)
        weight_grad(1, rows_in, gg)
        lines[1].send(0)
        weight_grad(2, rows_in, gu, {1: plane_two.middle})

        for n in range(tiles):
            down_streams[n].wait()
            if n + 1 < tiles:
                down_streams[n + 1].start()
            for lo in range(0, tile, 256):
                value = dot(act[...], wbuf[n % 2, 0, :, lo : lo + 256])
                r.part_out[:, n * tile + lo : n * tile + lo + 256] = value.astype(bf16)
        for copy, _ in pending[2][-2:]:
            copy.wait_send()
        for w in range(2, last):
            lines[0].forward(w)
        plane_two.end()

    big = 4 * tokens
    pl.run_scoped(
        ff_phase,
        pltpu.VMEM((big, width), bf16),
        pltpu.VMEM((big, ff), bf16),
        pltpu.VMEM((big, ff), bf16),
        pltpu.VMEM((big, ff), bf16),
        pltpu.VMEM((2, 384 // (2 * rb), 2, rb, ff), bf16),
        pltpu.VMEM((2, 2, ff, 512), bf16),
    )

    keys_step = 1024
    keys = r.kv.shape[2]
    key_steps = keys // keys_step
    scaling = hd ** (-0.5)
    small = r.small

    def attention_phase(
        hidden, cot, grad_hidden, branch, n1, q_v, ctx, dctx, rhs, gkv, dkv, dq, grad_one,
    ):
        loads = {}
        plane_out = PlaneSum(
            place, wires, r.part_out, r.out_fx, r.out_fy, r.out_lx, r.out_ly,
            (cot, branch),
        )
        o_parts, q_parts = r.o_parts, r.q_parts
        plane_o = PlaneSum(place, wires, o_parts, r.o_fx, r.o_fy, r.o_lx, r.o_ly)
        plane_q = PlaneSum(place, wires, q_parts, r.q_fx, r.q_fy, r.q_lx, r.q_ly)
        plane_w = PlaneSum(place, wires, r.w_parts, r.w_fx, r.w_fy, r.w_lx, r.w_ly)
        plane_out.begin()

        def load(name, src, dst):
            loads[name] = wires.copy(src, dst)
            loads[name].start()

        load("hidden", r.hidden, hidden)
        load("cot", r.cot, cot)
        load("ctx", r.ctx, ctx)
        load("q", r.q, q_v)
        load("n1", r.n1, n1)

        half = tokens // 2
        small[...] = jnp.zeros_like(small)

        def put(row, vector):
            for i in range(vector.shape[1] // 128):
                small[row + i : row + i + 1, :] = vector[:, i * 128 : (i + 1) * 128]

        def add_cores(full, core_land, parts):
            shares = []
            for b in range(4):
                shares.append(wires.remote(full.at[b, :, 1 - c], core_land.at[b], place.sibling))

            def finish():
                for b in range(4):
                    shares[b].wait_recv()
                    for i in range(chips):
                        lo = (b * chips + i) * rb
                        parts[lo : lo + rb, :] = full[b, i, c] + core_land[b, i]
                for copy in shares:
                    copy.wait_send()

            return shares, finish

        def out_projection(wo, fullo):
            load("wo0", r.wo, wo.at[0])
            load("wo1", r.wog, wo.at[pl.ds(1, 3)])
            loads["hidden"].wait()
            loads["cot"].wait()
            sums = jnp.zeros((1, width), f32)
            for i in range(2):
                here = pl.ds(i * half, half)
                grad = plane_two.value(here)
                hid = hidden[here, :]
                inv = lax.rsqrt(jnp.mean(hid * hid, axis=-1, keepdims=True) + epsilon)
                weighted = grad * r.pack[1:2, :]
                inner = jnp.mean(hid * weighted, axis=-1, keepdims=True)
                total = cot[here, :].astype(f32) + inv * weighted - hid * (inv * inv * inv * inner)
                grad_hidden[here, :] = total
                branch[here, :] = total.astype(bf16)
                sums = sums + jnp.sum(grad * hid * inv, axis=0, keepdims=True)
            put(12, sums)
            loads["ctx"].wait()
            shares, finish = add_cores(fullo, r.core_land, o_parts)
            for b in range(4):
                value = dot(branch[...], ctx[b], ((0,), (0,)))
                fullo[b] = value.astype(bf16).reshape(chips, 2, rb, qw)
                shares[b].start()
            loads["wo0"].wait()
            loads["wo1"].wait()
            for b in range(4):
                dctx[b] = dot(branch[...], wo[b], ((1,), (1,))).astype(bf16)
            finish()

        pl.run_scoped(
            out_projection,
            pltpu.VMEM((4, qw, width), bf16),
            pltpu.VMEM((4, chips, 2, rb, qw), bf16),
        )
        plane_o.begin()

        loads["q"].wait()
        dq[...] = jnp.zeros_like(dq)

        def scores_back(p_v, k_v, v_v):
            steps = 4 * key_steps
            sems = r.loop_sems

            def fetch(i):
                rem = (lambda a, b: a % b) if isinstance(i, int) else lax.rem
                kb, rh = i // 4, rem(i, 4)
                row, h = rh // 2, rem(rh, 2)
                slot = rem(i, 2)
                cols = pl.ds(pl.multiple_of(kb * keys_step, keys_step), keys_step)
                copies = [
                    pltpu.make_async_copy(r.kv.at[2 * h, row, cols], k_v.at[slot], sems.at[slot, 0]),
                    pltpu.make_async_copy(r.kv.at[2 * h + 1, row, cols], v_v.at[slot], sems.at[slot, 1]),
                    pltpu.make_async_copy(r.p.at[row, h, :, cols], p_v.at[slot, 0], sems.at[slot, 2]),
                    pltpu.make_async_copy(r.p.at[row, h + 2, :, cols], p_v.at[slot, 1], sems.at[slot, 3]),
                ]
                return copies

            for copy in fetch(0):
                copy.start()
            group = keys_step // (2 * span)

            def step(i, carry):
                kb, rh = i // 4, lax.rem(i, 4)
                row, h = rh // 2, lax.rem(rh, 2)
                slot = lax.rem(i, 2)

                @pl.when(i + 1 < steps)
                def _():
                    for copy in fetch(i + 1):
                        copy.start()

                for copy in fetch(i):
                    copy.wait()
                where = pl.ds(pl.multiple_of(row * span, span), span)
                grad_k = grad_v = None
                for g in range(2):
                    b = h + 2 * g
                    queries = q_v[b, row].reshape(heads * span, hd)
                    outs = dctx[b, where, :]
                    ctxs = ctx[b, where, :]
                    go = jnp.concatenate([outs[:, n * hd : (n + 1) * hd] for n in range(heads)], axis=0)
                    co = jnp.concatenate([ctxs[:, n * hd : (n + 1) * hd] for n in range(heads)], axis=0)
                    inner = jnp.sum(go.astype(f32) * co.astype(f32), axis=-1, keepdims=True)
                    grad_probs = dot(go, v_v[slot], ((1,), (1,)))
                    probs = p_v[slot, g]
                    grad_scores = (probs.astype(f32) * (grad_probs - inner)).astype(bf16)
                    dq[b, row] += dot(grad_scores, k_v[slot])
                    gk = dot(grad_scores, queries, ((0,), (0,)))
                    gv = dot(probs, go, ((0,), (0,)))
                    grad_k = gk if g == 0 else grad_k + gk
                    grad_v = gv if g == 0 else grad_v + gv
                zs = pl.ds(kb * group, group)
                krows = pl.ds(pl.multiple_of((4 * h + row) * span, span), span)
                vrows = pl.ds(pl.multiple_of((4 * h + 2 + row) * span, span), span)
                dkv[zs, :, krows, :] = (grad_k * scaling).astype(bf16).reshape(group, 2, span, hd)
                dkv[zs, :, vrows, :] = grad_v.astype(bf16).reshape(group, 2, span, hd)
                return carry

            lax.fori_loop(0, steps, step, 0)

        cosine, sine = r.cos, r.sin
        save_out = wires.copy(cot, r.output)

        def keys_and_queries(wq, wkv, o_rooms):
            plane_o.rooms = (o_rooms.at[0], o_rooms.at[1])
            load("wq0", r.wq, wq.at[0])
            load("wq1", r.wqg, wq.at[pl.ds(1, 3)])
            load("wk", r.wk, wkv.at[0, :, pl.ds(0, hd)])
            load("wv", r.wv, wkv.at[0, :, pl.ds(hd, hd)])
            load("wkv1", r.wkvg, wkv.at[1])
            pl.run_scoped(
                scores_back,
                pltpu.VMEM((2, 2, heads * span, keys_step), bf16),
                pltpu.VMEM((2, keys_step, hd), bf16),
                pltpu.VMEM((2, keys_step, hd), bf16),
            )

            share_kv = wires.remote(dkv.at[:, 1 - c], r.kv_core, place.sibling)
            room = r.kv_room
            line_kv = LineSumDown(place, wires, lambda d: dkv.at[d, c], r.kv_land, room.at[0])
            share_kv.start()
            for b in range(4):
                for row in range(2):
                    here = pl.ds(row * span, span)
                    for n in range(heads):
                        part = dq[b, row, n * span : (n + 1) * span, :] * scaling
                        part = turn(part, cosine[here, :], -sine[here, :])
                        rhs[b, here, n * hd : (n + 1) * hd] = part.astype(bf16)
            for name in ("wq0", "wq1", "wk", "wv", "wkv1", "n1"):
                loads[name].wait()

            def query_part(fullq):
                shares, finish = add_cores(fullq, r.core_land, q_parts)
                for b in range(4):
                    fullq[b] = dot(n1[...], rhs[b], ((0,), (0,))).astype(bf16).reshape(chips, 2, rb, qw)
                share_kv.wait_recv()
                for i in range(0, chips, 2):
                    wires.fetch([r.kv_core.at[i], r.kv_core.at[i + 1]], [room.at[0], room.at[1]])
                    add_rows(dkv.at[i, c], room.at[0])
                    add_rows(dkv.at[i + 1, c], room.at[1])
                for w in range(last):
                    line_kv.send(w)
                for w in range(1, last):
                    lines[1].send(w)
                for copy in shares:
                    copy.start()
                grad_one[...] = dot(rhs[0], wq[0], ((1,), (1,)))
                if last > 1:
                    lines[1].forward(1)
                    line_kv.forward(1)
                finish()

            pl.run_scoped(query_part, pltpu.VMEM((4, chips, 2, rb, qw), bf16))
            plane_q.begin()
            plane_o.middle()
            for w in range(2, last):
                line_kv.forward(w)
            for b in range(1, 4):
                grad_one[...] += dot(rhs[b], wq[b], ((1,), (1,)))
            line_kv.finish()
            mine = dkv.at[z, c]
            for h in range(2):
                gk = mine[2 * h * 2 * span : (2 * h + 1) * 2 * span, :].astype(f32)
                gkv[h, :, :hd] = turn(gk, cosine[...], -sine[...]).astype(bf16)
                gkv[h, :, hd:] = mine[(2 * h + 1) * 2 * span : (2 * h + 2) * 2 * span, :]
            mypart = pl.ds(pl.multiple_of(place.qh * hd, hd), hd)
            otherpart = pl.ds(pl.multiple_of((1 - place.qh) * hd, hd), hd)

            def key_part(fullw):
                shares, finish = add_cores(fullw, r.w_core, r.w_parts)
                for b in range(4):
                    value = dot(n1[...], gkv[b % 2, :, mypart if b < 2 else otherpart], ((0,), (0,)))
                    fullw[b] = value.astype(bf16).reshape(chips, 2, rb, hd)
                    shares[b].start()
                for h in range(2):
                    grad_one[...] += dot(gkv[h], wkv[h], ((1,), (1,)))
                finish()

            pl.run_scoped(key_part, pltpu.VMEM((4, chips, 2, rb, hd), bf16))
            plane_w.begin()
            share_kv.wait_send()

        pl.run_scoped(
            keys_and_queries,
            pltpu.VMEM((4, width, qw), bf16),
            pltpu.VMEM((2, width, 2 * hd), bf16),
            pltpu.VMEM((2, chips * rb, qw), bf16),
        )
        tok = n1
        load("tok", r.tok, tok)

        def tail(tok_ref, o_rooms, q_rooms, w_rooms, line_o_sum, line_q_sum, line_w_sum):
            plane_o.rooms = (o_rooms.at[0], o_rooms.at[1])
            plane_q.rooms = (q_rooms.at[0], q_rooms.at[1])
            plane_w.rooms = (w_rooms.at[0], w_rooms.at[1])
            loads["tok"].wait()
            sums = jnp.zeros((1, width), f32)
            for i in range(2):
                here = pl.ds(i * half, half)
                grad = grad_one[here, :]
                tok = tok_ref[here, :].astype(f32)
                inv = lax.rsqrt(jnp.mean(tok * tok, axis=-1, keepdims=True) + epsilon)
                weighted = grad * r.pack[0:1, :]
                inner = jnp.mean(tok * weighted, axis=-1, keepdims=True)
                grad_hidden[here, :] += inv * weighted - tok * (inv * inv * inv * inner)
                sums = sums + jnp.sum(grad * tok * inv, axis=0, keepdims=True)
            save_tokens = wires.copy(grad_hidden, r.tokens_grad)
            save_tokens.start()
            put(0, sums)
            k, q = place.kv, place.qh
            canonical = [2 * k + q, 2 * (1 - k) + q, 2 * k + 1 - q, 2 * (1 - k) + 1 - q]
            for b in range(4):
                total = jnp.sum(rhs[b].astype(f32), axis=0, keepdims=True)
                for n in range(heads):
                    small[pl.ds(24 + canonical[b] * heads + n, 1), :] = total[:, n * hd : (n + 1) * hd]
            for h in range(2):
                total = jnp.sum(gkv[h].astype(f32), axis=0, keepdims=True)
                head = k if h == 0 else 1 - k
                small[pl.ds(36 + 2 * head, 1), :] = total[:, :hd]
                small[pl.ds(37 + 2 * head, 1), :] = total[:, hd:]

            plane_q.middle()
            plane_w.middle()
            plane_out.middle()
            spread_sums = []
            for totals, land in ((line_w_sum, r.w_land), (line_o_sum, r.o_land), (line_q_sum, r.q_land)):
                spread_sums.append(Spread(place, wires, lambda d, t=totals: t.at[d], lambda d, t=land: t.at[d]))
            spread_w, spread_o, spread_q = spread_sums
            lines[2].send(0)
            for plane, spread, totals in (
                (plane_o, spread_o, line_o_sum),
                (plane_q, spread_q, line_q_sum),
                (plane_w, spread_w, line_w_sum),
            ):
                plane.end()
                for i in range(chips):
                    totals[i] = plane.value(pl.ds(i * rb, rb)).astype(bf16)
                if spread is not spread_q:
                    spread.send()
            spread_q.send()
            for w in range(1, last - 1):
                lines[2].send(w)
            for w in range(2, last):
                lines[1].forward(w)
            plane_out.end()
            for i in range(2):
                here = pl.ds(i * half, half)
                cot[here, :] = (hidden[here, :] + plane_out.value(here)).astype(bf16)
            save_out.start()

            buffers = r.small_land
            for j, device in enumerate([place.sibling, place.across_x, place.across_y]):
                copy = wires.remote(small, buffers.at[j], device)
                copy.start()
                copy.wait_recv()
                copy.wait_send()
                small[...] += buffers[j]
            smalls = r.smalls
            smalls[z] = small[...]
            lines[0].finish()
            spread_w.receive(lambda d: add_rows(line_w_sum.at[z], r.w_land.at[d]))

            kvall = r.kvall
            r.kv_own[...] = line_w_sum[z]
            mycols = pl.ds(pl.multiple_of(k * hd, hd), hd)

            def piece(chip):
                return kvall.at[q, chip, c, :, mycols]

            own = wires.copy(r.kv_own, piece(z))
            own.start()
            own.wait()

            spread_pieces = Spread(place, wires, lambda d: r.kv_own, piece)
            spread_smalls = Spread(place, wires, lambda d: small, lambda d: smalls.at[d])
            spread_pieces.send()
            spread_smalls.send()
            lines[2].send(last - 1)
            lines[1].finish()
            for w in range(1, last - 1):
                lines[2].forward(w)
            spread_o.receive(lambda d: add_rows(line_o_sum.at[z], r.o_land.at[d]))
            spread_q.receive(lambda d: add_rows(line_q_sum.at[z], r.q_land.at[d]))
            save_o = wires.copy(line_o_sum.at[z], r.o_out)
            save_q = wires.copy(line_q_sum.at[z], r.q_out)
            save_o.start()
            save_q.start()
            spread_pieces.receive()
            spread_smalls.receive()

            def quarter(part, cols, lo, count):
                return kvall.at[part, pl.ds(lo, count), c, :, cols]

            othercols = pl.ds(pl.multiple_of((1 - k) * hd, hd), hd)
            hc = chips // 2
            across_x = wires.remote(quarter(q, mycols, 0, chips), quarter(q, mycols, 0, chips), place.across_x)
            across_y = wires.remote(quarter(q, mycols, 0, chips), quarter(q, mycols, 0, chips), place.across_y)
            relay_x = wires.remote(quarter(1 - q, mycols, 0, hc), quarter(1 - q, mycols, 0, hc), place.across_x)
            relay_y = wires.remote(quarter(q, othercols, hc, hc), quarter(q, othercols, hc, hc), place.across_y)
            across_x.start()
            across_y.start()
            across_y.wait_recv()
            relay_x.start()
            across_x.wait_recv()
            relay_y.start()
            relay_x.wait_recv()
            relay_y.wait_recv()
            share = wires.remote(kvall.at[:, :, c], kvall.at[:, :, c], place.sibling)
            share.start()
            lines[2].forward(last - 1)
            for spread in spread_sums + [spread_pieces, spread_smalls]:
                spread.drain()

            total = smalls[0]
            for i in range(1, chips):
                total = total + smalls[i]
            smalls[0] = total
            save_small = wires.copy(smalls.at[0], r.small_out)
            save_small.start()
            lines[2].finish()
            save_ff = [wires.copy(ffsum.at[m, z], r.ff_out.at[m]) for m in range(3)]
            for copy in save_ff:
                copy.start()

            share.wait_recv()
            for copy in (across_x, across_y, relay_x, relay_y, share):
                copy.wait_send()
            for copy in save_ff + [save_tokens, save_small, save_q, save_o]:
                copy.wait()

        pl.run_scoped(
            functools.partial(tail, tok),
            pltpu.VMEM((2, chips * rb, qw), bf16),
            pltpu.VMEM((2, chips * rb, qw), bf16),
            pltpu.VMEM((2, chips * rb, hd), bf16),
            pltpu.VMEM((chips, rb, qw), bf16),
            pltpu.VMEM((chips, rb, qw), bf16),
            pltpu.VMEM((chips, rb, hd), bf16),
        )
        save_out.wait()

    pl.run_scoped(
        attention_phase,
        pltpu.VMEM((tokens, width), f32),
        pltpu.VMEM((tokens, width), bf16),
        pltpu.VMEM((tokens, width), f32),
        pltpu.VMEM((tokens, width), bf16),
        pltpu.VMEM((tokens, width), bf16),
        pltpu.VMEM((4, 2, heads, span, hd), bf16),
        pltpu.VMEM((4, tokens, qw), bf16),
        pltpu.VMEM((4, tokens, qw), bf16),
        pltpu.VMEM((4, tokens, qw), bf16),
        pltpu.VMEM((2, tokens, 2 * hd), bf16),
        pltpu.VMEM((chips, 2, 8 * span, hd), bf16),
        pltpu.VMEM((4, 2, heads * span, hd), f32),
        pltpu.VMEM((tokens, width), f32),
    )


def back(seq_size, operands, whole_rows):
    shape = jax.ShapeDtypeStruct
    ops = types.SimpleNamespace(**operands)
    chips = seq_size // 2
    tokens, width = ops.tok.shape
    ff = ops.wg.shape[0]
    span = tokens // 2
    hd = ops.cos.shape[1]
    qw = ops.wq.shape[1]
    rb = width // (2 * chips)
    part = chips * rb
    in_vmem = [id(a) for a in (ops.pack, ops.cos, ops.sin)]
    outs = dict(
        output=shape((tokens, width), bf16),
        tokens_grad=shape((tokens, width), f32),
        ff_out=shape((3, rb, ff), bf16),
        q_out=shape((rb, qw), bf16),
        o_out=shape((rb, qw), bf16),
        kvall=shape((2, chips, 2, rb, 2 * hd), bf16),
        small_out=shape((40, 128), f32),
        ffland=shape((3, 2, chips, rb, ff), bf16),
        kv_land=shape((chips, 8 * span, hd), bf16),
    )
    v = pltpu.VMEM
    scratch = dict(
        ffsum=v((3, chips, rb, ff), bf16),
        ffroom=v((rb, ff), bf16),
        part_two=v((4 * tokens, width), bf16),
        part_out=v((4 * tokens, width), bf16),
    )
    scratch.update(o_land=v((chips, rb, qw), bf16))
    scratch.update(q_land=v((chips, rb, qw), bf16))
    scratch.update(w_land=v((chips, rb, hd), bf16))
    scratch.update(two_fx=v((tokens // 2, width), bf16))
    scratch.update(two_fy=v((tokens // 2, width), bf16))
    scratch.update(two_lx=v((tokens, width), bf16))
    scratch.update(two_ly=v((tokens, width), bf16))
    for name, rows, w in (("out", tokens, width), ("o", part, qw), ("q", part, qw), ("w", part, hd)):
        outs[name + "_fx"] = shape((rows // 2, w), bf16)
        outs[name + "_fy"] = shape((rows // 2, w), bf16)
        outs[name + "_lx"] = shape((rows, w), bf16)
        outs[name + "_ly"] = shape((rows, w), bf16)
    for name, w in (("o", qw), ("q", qw), ("w", hd)):
        scratch[name + "_parts"] = v((4 * part, w), bf16)
    scratch.update(core_land=v((4, chips, rb, qw), bf16))
    scratch.update(w_core=v((4, chips, rb, hd), bf16))
    outs.update(kv_core=shape((chips, 8 * span, hd), bf16))
    scratch.update(kv_room=v((2, 8 * span, hd), bf16))
    scratch.update(small=v((40, 128), f32))
    scratch.update(small_land=v((3, 40, 128), f32))
    scratch.update(smalls=v((chips, 40, 128), f32))
    scratch.update(kv_own=v((rb, hd), bf16))
    scratch.update(loop_sems=pltpu.SemaphoreType.DMA((2, 4)))
    last = chips - 1
    remotes = 3 * 2 * last + 12 + 12 + 8 + 9 + last + 4 * last + 12 + 4 * last + 8 + 12 + 10 + 5 * chips
    scratch.update(send=pltpu.SemaphoreType.DMA((remotes,)))
    scratch.update(recv=pltpu.SemaphoreType.DMA((remotes,)))
    scratch.update(local=pltpu.SemaphoreType.DMA((64,)))
    names = list(operands) + list(outs) + list(scratch)
    results = pl.pallas_call(
        functools.partial(back_kernel, seq_size, names),
        out_shape=tuple(outs.values()),
        in_specs=[VMEM if id(a) in in_vmem else ANY for a in operands.values()],
        out_specs=tuple([ANY] * len(outs)),
        scratch_shapes=list(scratch.values()),
        name="weight_gradients_and_attention_back",
        compiler_params=pltpu.CompilerParams(
            collective_id=1, has_side_effects=True, vmem_limit_bytes=62 * 2**20
        ),
    )(*operands.values())
    return types.SimpleNamespace(**dict(zip(outs, results)))


def last_kernel(names, *refs):
    r = types.SimpleNamespace(**dict(zip(names, refs)))
    local = r.local
    count = [0]

    def copy(src, dst):
        made = pltpu.make_async_copy(src, dst, local.at[count[0]])
        count[0] += 1
        made.start()
        return made

    passed = [
        (copy(r.output, r.out_in), r.out_in, r.output_to),
        (copy(r.tokens_grad, r.tokens_in), r.tokens_in, r.tokens_to),
    ]
    jobs = []
    for m in range(3):
        jobs.append((r.ff_out.at[m], r.ff_in.at[m], r.ff_wide.at[m], (r.ff0_to, r.ff1_to, r.ff2_to)[m], None))
    jobs.append((r.kvall, r.kv_in, r.kv_wide, None, None))
    jobs.append((r.q_out, r.q_in, r.q_wide, r.q_to, None))
    jobs.append((r.o_out, r.o_in, r.o_wide, r.o_to, None))
    loads = [copy(src, room) for src, room, _, _, _ in jobs]
    for i in range(12):
        r.gain_one_to[i * 128 : (i + 1) * 128] = r.small_out[i, :]
        r.gain_two_to[i * 128 : (i + 1) * 128] = r.small_out[12 + i, :]
        r.query_bias_to[i * 128 : (i + 1) * 128] = r.small_out[24 + i, :]
    for i in range(2):
        r.key_bias_to[i * 128 : (i + 1) * 128] = r.small_out[36 + 2 * i, :]
        r.value_bias_to[i * 128 : (i + 1) * 128] = r.small_out[37 + 2 * i, :]
    stores = []
    for load, room, target in passed:
        load.wait()
        stores.append(copy(room, target))
    for load, (_, room, wide, target, _) in zip(loads, jobs):
        load.wait()
        if target is None:
            wide[...] = room[...].astype(f32)
            stores.append(copy(wide.at[0], r.key_to))
            stores.append(copy(wide.at[1], r.value_to))
        else:
            wide[...] = room[:, : wide.shape[1]].astype(f32)
            stores.append(copy(wide, target))
    for made in stores:
        made.wait()


def last(made, qw, hd):
    shape = jax.ShapeDtypeStruct
    rb, ff = made.ff_out.shape[1:]
    kvall = made.kvall.reshape(2, -1, 2 * hd)
    width = kvall.shape[1]
    ins = dict(
        output=made.output, tokens_grad=made.tokens_grad, ff_out=made.ff_out, q_out=made.q_out, o_out=made.o_out, kvall=kvall,
        small_out=made.small_out,
    )
    outs = dict(
        output_to=made.output,
        tokens_to=made.tokens_grad,
        ff0_to=shape((rb, ff), f32),
        ff1_to=shape((rb, ff), f32),
        ff2_to=shape((rb, ff), f32),
        q_to=shape((rb, qw), f32),
        o_to=shape((rb, qw), f32),
        key_to=shape((width, 2 * hd), f32),
        value_to=shape((width, 2 * hd), f32),
        gain_one_to=shape((width,), f32),
        gain_two_to=shape((width,), f32),
        query_bias_to=shape((width,), f32),
        key_bias_to=shape((2 * hd,), f32),
        value_bias_to=shape((2 * hd,), f32),
    )
    v = pltpu.VMEM
    scratch = dict(
        out_in=v(made.output.shape, bf16),
        tokens_in=v(made.tokens_grad.shape, f32),
        ff_in=v((3, rb, ff), bf16),
        ff_wide=v((3, rb, ff), f32),
        kv_in=v(kvall.shape, bf16),
        kv_wide=v(kvall.shape, f32),
        q_in=v((rb, qw), bf16),
        q_wide=v((rb, qw), f32),
        o_in=v((rb, qw), bf16),
        o_wide=v((rb, qw), f32),
        local=pltpu.SemaphoreType.DMA((20,)),
    )
    in_vmem = [n for n in outs if outs[n].ndim == 1]
    results = pl.pallas_call(
        functools.partial(last_kernel, list(ins) + list(outs) + list(scratch)),
        out_shape=tuple(shape(o.shape, o.dtype) for o in outs.values()),
        in_specs=[VMEM if a is made.small_out else ANY for a in ins.values()],
        out_specs=tuple(VMEM if n in in_vmem else ANY for n in outs),
        scratch_shapes=list(scratch.values()),
        name="results",
        compiler_params=pltpu.CompilerParams(vmem_limit_bytes=62 * 2**20),
    )(*ins.values())
    return types.SimpleNamespace(**dict(zip(outs, results)))


def local(
    seq_size,
    tokens, attn_gain, query_weight, query_bias, key_matrix, key_offset_bias, value_matrix, value_offset_bias, out_weight,
    mlp_gain, gate_weight, up_weight, down_weight, segment_ids, position_ids, cotangent,
):
    rows, span, width = tokens.shape
    count = rows * span
    hd = key_matrix.shape[1]
    qw = query_weight.shape[1]
    heads = qw // hd
    k, q, s = lax.axis_index("kv"), lax.axis_index("qh"), lax.axis_index("seq")
    row_start = (2 * k + q) * rows
    positions = lax.dynamic_slice_in_dim(position_ids, row_start, rows, 0)
    inverse = 1.0 / jnp.power(rope_base, jnp.arange(hd // 2, dtype=f32) * 2.0 / hd)
    inverse = jnp.concatenate([inverse, inverse])
    phase = positions.astype(f32).reshape(count, 1) * inverse
    cosine = jnp.cos(phase)
    sine = jnp.sin(phase) * jnp.where(jnp.arange(hd) < hd // 2, -1.0, 1.0)
    tok = tokens.reshape(count, width)
    cot = cotangent.reshape(count, width)
    bias = jnp.concatenate([query_bias, key_offset_bias, value_offset_bias])
    bias = jnp.pad(bias, (0, width - bias.shape[0]))
    pack = jnp.pad(jnp.stack([attn_gain, mlp_gain, bias]).astype(f32), ((0, 5), (0, 0)))
    gate_rows, up_rows = gate_weight.T, up_weight.T
    wqg, wog, wkvg, x2g, cotg, hidden, n1, qrot, kv, probs, ctx, act, gg, gu = front(
        seq_size, tok, cot, pack, query_weight, key_matrix, value_matrix, out_weight, cosine, sine, segment_ids,
        gate_rows, up_rows, down_weight,
    )
    made = back(
        seq_size,
        dict(
            x2g=x2g.reshape(4 * count, width), cotg=cotg.reshape(4 * count, width), act=act, gg=gg, gu=gu, wg=gate_rows,
            wu=up_rows, wd=down_weight, hidden=hidden, tok=tok, cot=cot, pack=pack, cos=cosine, sin=sine, n1=n1, q=qrot,
            kv=kv, p=probs, ctx=ctx, wq=query_weight, wqg=wqg, wo=out_weight, wog=wog, wk=key_matrix, wv=value_matrix,
            wkvg=wkvg,
        ),
        rows,
    )
    made = last(made, qw, hd)
    return (
        made.output_to.reshape(tokens.shape),
        made.tokens_to.reshape(tokens.shape),
        made.gain_one_to,
        made.q_to,
        made.query_bias_to,
        made.key_to,
        made.key_bias_to,
        made.value_to,
        made.value_bias_to,
        made.o_to.T,
        made.gain_two_to,
        made.ff1_to,
        made.ff2_to,
        made.ff0_to.T,
    )


def solution(mesh):
    return jax.shard_map(
        functools.partial(local, mesh.shape["seq"]),
        mesh=mesh,
        in_specs=(
            P(("kv", "qh"), "seq", None),
            P(),
            P(None, ("kv", "qh")),
            P(("kv", "qh")),
            P(None, "kv"),
            P("kv"),
            P(None, "kv"),
            P("kv"),
            P(("kv", "qh"), None),
            P(),
            P(None, ("kv", "qh")),
            P(None, ("kv", "qh")),
            P(("kv", "qh"), None),
            P(),
            P(None, "seq"),
            P(("kv", "qh"), "seq", None),
        ),
        out_specs=(
            P(("kv", "qh"), "seq", None),
            P(("kv", "qh"), "seq", None),
            P(),
            P("seq", ("kv", "qh")),
            P(),
            P(),
            P(),
            P(),
            P(),
            P(("kv", "qh"), "seq"),
            P(),
            P("seq", ("kv", "qh")),
            P("seq", ("kv", "qh")),
            P(("kv", "qh"), "seq"),
        ),
        check_vma=False,
    )
```

profile of v0, /device:TPU:0, one launch (start us, length us, event | category | flops | bytes accessed | tf_op | source)
XLA Modules:
  0.0 388.7 jit_solution(1140986883282678626)
XLA Ops:
  0.7 0.7 convert_bitcast_fusion
  1.4 0.1 compare_select_fusion
  1.4 0.7 fusion.11
  2.2 0.7 stack.12
  2.9 0.7 stack.13
  3.6 0.6 fusion.6.pack_ref.refs_11_
  4.2 1.2 fusion
  5.4 120.0 %attention_front.1 = (bf16[3,1536,384]{2,1,0:T(8,128)(2,1)}, bf16[3,384,1536]{2,1,0:T(8,128)(2,1)}, bf16[1536,256]{1,0:T(8,128)(2,1)}, bf16[4,256,1536]{2,1,0:T(...) custom-call(bf16[256,1536]{1,0:T(8,128)(2,1)} %bitcast.17, ...), custom_call_target="tpu_custom_call" | custom-call | tf_op jit(solution)/shard_map/attention_front/pallas_call | solution.py:534
  125.4 254.6 %weight_gradients_and_attention_back.1 = (bf16[256,1536]{1,0:T(8,128)(2,1)}, f32[256,1536]{1,0:T(8,128)}, bf16[3,192,2240]{2,1,0:T(8,128)(2,1)}, bf16[192,384]{1...) custom-call(bf16[1024,1536]{1,0:T(8,128)(2,1)} %bitcast.21, ...), custom_call_target="tpu_custom_call" | custom-call | tf_op jit(solution)/shard_map/weight_gradients_and_attention_back/pallas_call | solution.py:1370
  380.0 8.2 %results.1 = (bf16[256,1536]{1,0:T(8,128)(2,1)}, f32[256,1536]{1,0:T(8,128)}, f32[192,2240]{1,0:T(8,128)}, f32[192,2240]{1,0:T(8,128)}, f32[192,2240]{1,0:T(8,12...) custom-call(bf16[256,1536]{1,0:T(8,128)(2,1)} %get-tuple-element.63., ...), custom_call_target="tpu_custom_call" | custom-call | tf_op jit(solution)/shard_map/results/pallas_call | solution.py:1470
  (2 shorter events, 0.0 us)
where the time goes:
time: 393 us; the launch traced here: 389 us
  Pallas kernels  383 us (97%)
    pallas_call x1, Pallas kernels, back(): pl.pallas_call(functools.partial(back_kernel, seq_size, names), out_shape...  255 us
    pallas_call x1, Pallas kernels, front(): pl.pallas_call(functools.partial(front_kernel, seq_size), out_shape=outs,...  120 us
    pallas_call x1, Pallas kernels, last(): pl.pallas_call(functools.partial(last_kernel, list(ins) + list(outs) + li...  8.2 us

commit v1 on v0

--- a/solution.py
+++ b/solution.py
@@ -138,6 +138,59 @@
             copy.wait_send()
 
 
+class PairGather:
+    def __init__(self, place, wires, own, gathered):
+        rows = own.shape[0]
+        quarter, eighth = rows // 4, rows // 8
+        odd = lax.rem(place.chip, 2)
+        pair = (place.kv, place.qh, place.seq + 2 - 4 * odd)
+        base = (2 * place.core + odd) * quarter
+        mine = pl.ds(pl.multiple_of(base, quarter), quarter)
+        first = pl.ds(pl.multiple_of(base, eighth), eighth)
+        second = pl.ds(pl.multiple_of(base + eighth, eighth), eighth)
+        theirs = pl.ds(pl.multiple_of((2 * place.core + 1 - odd) * quarter, quarter), quarter)
+        g = gathered
+        self.x = wires.remote(own.at[mine], g.at[0, mine], place.across_x)
+        self.y = wires.remote(own.at[mine], g.at[1, mine], place.across_y)
+        self.dx = wires.remote(g.at[1, first], g.at[2, first], place.across_x)
+        self.dy = wires.remote(g.at[0, second], g.at[2, second], place.across_y)
+        pieces = [g.at[0, mine], g.at[1, mine], g.at[2, first], g.at[2, second]]
+        self.to_pair = [wires.remote(piece, piece, pair) for piece in pieces]
+        self.share = [wires.remote(piece, piece, place.sibling) for piece in pieces]
+        self.pass_on = [wires.remote(g.at[i, theirs], g.at[i, theirs], place.sibling) for i in range(3)]
+
+    def got(self, copy, i):
+        copy.wait_recv()
+        self.to_pair[i].start()
+        self.share[i].start()
+
+    def got_x(self):
+        self.got(self.x, 0)
+        self.dy.start()
+
+    def got_y(self):
+        self.got(self.y, 1)
+        self.dx.start()
+
+    def got_diagonal(self):
+        self.got(self.dx, 2)
+        self.got(self.dy, 3)
+
+    def got_pair(self, block):
+        for i in ((0,), (1,), (2, 3))[block]:
+            self.to_pair[i].wait_recv()
+        self.pass_on[block].start()
+
+    def complete(self, block):
+        for i in ((0,), (1,), (2, 3))[block]:
+            self.share[i].wait_recv()
+        self.pass_on[block].wait_recv()
+
+    def drain(self):
+        for copy in [self.x, self.y, self.dx, self.dy] + self.to_pair + self.share + self.pass_on:
+            copy.wait_send()
+
+
 class TokenGather:
     def __init__(self, place, wires, own, gathered):
         half = own.shape[0] // 2
@@ -194,9 +247,10 @@
 
     kv_v[...] = jnp.zeros_like(kv_v)
     barrier = greet(
-        [place.across_x, place.across_y, place.diagonal, place.sibling], [(place.has_below, place.below)]
+        [place.across_x, place.across_y, place.diagonal, place.sibling],
+        [(place.has_below, place.below), (place.has_above, place.above)],
     )
-    pl.semaphore_wait(barrier, 4 + jnp.where(place.has_above, 1, 0))
+    pl.semaphore_wait(barrier, 4 + jnp.where(place.has_above, 1, 0) + jnp.where(place.has_below, 1, 0))
 
     half = width // 2
     mine = pl.ds(pl.multiple_of(place.core * half, half), half)
@@ -210,7 +264,7 @@
         for i, device in enumerate((place.across_x, place.across_y, place.diagonal))
     ]
     gq = WeightGather(place, wires, wq_ref, wqg_v)
-    go = WeightGather(place, wires, wo_ref, wog_v)
+    go = PairGather(place, wires, wo_ref, wog_v)
     for copy in kvx + packed:
         copy.start()
     gq.begin()
@@ -366,11 +420,13 @@
                 pltpu.make_async_copy(p_v.at[i % 2], p_ref.at[r, i], p_sems.at[i % 2]).wait()
 
         go.got_y()
-        attend(0)
         go.got_x()
         gather_cot.begin()
+        attend(0)
+        go.got_diagonal()
         attend(1)
-        go.got_diagonal()
+        go.got_pair(0)
+        go.got_pair(1)
         save_n1.wait()
         save_q.wait()
 
@@ -392,6 +448,8 @@
         load_o.wait()
         hidden_v[...] = tok_ref[...].astype(f32) + dot(ctx_v[0], wo_v[...])
         for i in (1, 2, 3):
+            if i == 3:
+                go.got_pair(2)
             go.complete(i - 1)
             hidden_v[...] += dot(ctx_v[i], wog_v[i - 1])
         hidden = hidden_v[...]
@@ -515,7 +573,7 @@
         shape((4 * tokens, ff), bf16),
         shape((4 * tokens, ff), bf16),
     )
-    remotes = 6 + 8 + 8 + 2 * chips + 8
+    remotes = 6 + 8 + 15 + 2 * chips + 8
     scratch = [
         pltpu.VMEM((3,) + pack.shape, f32),
         pltpu.VMEM((4, 2, keys, hd), bf16),
@@ -1093,11 +1151,11 @@
                     line_kv.send(w)
                 for w in range(1, last):
                     lines[1].send(w)
+                lines[2].send(0)
                 for copy in shares:
                     copy.start()
                 grad_one[...] = dot(rhs[0], wq[0], ((1,), (1,)))
                 if last > 1:
-                    lines[1].forward(1)
                     line_kv.forward(1)
                 finish()
 
@@ -1106,6 +1164,8 @@
             plane_o.middle()
             for w in range(2, last):
                 line_kv.forward(w)
+            if last > 1:
+                lines[1].forward(1)
             for b in range(1, 4):
                 grad_one[...] += dot(rhs[b], wq[b], ((1,), (1,)))
             line_kv.finish()
@@ -1177,20 +1237,12 @@
             for totals, land in ((line_w_sum, r.w_land), (line_o_sum, r.o_land), (line_q_sum, r.q_land)):
                 spread_sums.append(Spread(place, wires, lambda d, t=totals: t.at[d], lambda d, t=land: t.at[d]))
             spread_w, spread_o, spread_q = spread_sums
-            lines[2].send(0)
-            for plane, spread, totals in (
-                (plane_o, spread_o, line_o_sum),
-                (plane_q, spread_q, line_q_sum),
-                (plane_w, spread_w, line_w_sum),
-            ):
+            for plane, totals in ((plane_w, line_w_sum), (plane_o, line_o_sum), (plane_q, line_q_sum)):
                 plane.end()
                 for i in range(chips):
                     totals[i] = plane.value(pl.ds(i * rb, rb)).astype(bf16)
-                if spread is not spread_q:
-                    spread.send()
-            spread_q.send()
-            for w in range(1, last - 1):
-                lines[2].send(w)
+            for spread in spread_sums:
+                spread.send()
             for w in range(2, last):
                 lines[1].forward(w)
             plane_out.end()
@@ -1226,7 +1278,8 @@
             spread_smalls = Spread(place, wires, lambda d: small, lambda d: smalls.at[d])
             spread_pieces.send()
             spread_smalls.send()
-            lines[2].send(last - 1)
+            for w in range(1, last):
+                lines[2].send(w)
             lines[1].finish()
             for w in range(1, last - 1):
                 lines[2].forward(w)

time: 393 us -> 372 us (0.947)
  Pallas kernels: 383 us -> 362 us
    pallas_call x1, Pallas kernels: 120 us -> 109 us  [front(): pl.pallas_call(functools.partial(front_kernel, seq_size), out_shape=outs,...]
    pallas_call x1, Pallas kernels: 255 us -> 244 us  [back(): pl.pallas_call(functools.partial(back_kernel, seq_size, names), out_shape...]
where the time goes in v1:
time: 372 us; the launch traced here: 368 us
  Pallas kernels  362 us (97%)
    pallas_call x1, Pallas kernels, back(): pl.pallas_call(functools.partial(back_kernel, seq_size, names), out_shape...  244 us
    pallas_call x1, Pallas kernels, front(): pl.pallas_call(functools.partial(front_kernel, seq_size), out_shape=outs,...  109 us
    pallas_call x1, Pallas kernels, last(): pl.pallas_call(functools.partial(last_kernel, list(ins) + list(outs) + li...  8.2 us

profile of v1, /device:TPU:0, one launch (start us, length us, event | category | flops | bytes accessed | tf_op | source)
XLA Modules:
  0.0 367.7 jit_solution(17424842151126073910)
XLA Ops:
  0.7 0.7 convert_bitcast_fusion
  1.4 0.1 compare_select_fusion
  1.4 0.7 fusion.11
  2.2 0.7 stack.12
  2.9 0.7 stack.13
  3.6 0.6 fusion.6.pack_ref.refs_11_
  4.2 1.2 fusion
  5.4 109.2 %attention_front.1 = (bf16[3,1536,384]{2,1,0:T(8,128)(2,1)}, bf16[3,384,1536]{2,1,0:T(8,128)(2,1)}, bf16[1536,256]{1,0:T(8,128)(2,1)}, bf16[4,256,1536]{2,1,0:T(...) custom-call(bf16[256,1536]{1,0:T(8,128)(2,1)} %bitcast.17, ...), custom_call_target="tpu_custom_call" | custom-call | tf_op jit(solution)/shard_map/attention_front/pallas_call | solution.py:592
  114.6 244.3 %weight_gradients_and_attention_back.1 = (bf16[256,1536]{1,0:T(8,128)(2,1)}, f32[256,1536]{1,0:T(8,128)}, bf16[3,192,2240]{2,1,0:T(8,128)(2,1)}, bf16[192,384]{1...) custom-call(bf16[1024,1536]{1,0:T(8,128)(2,1)} %bitcast.21, ...), custom_call_target="tpu_custom_call" | custom-call | tf_op jit(solution)/shard_map/weight_gradients_and_attention_back/pallas_call | solution.py:1423
  359.0 8.2 %results.1 = (bf16[256,1536]{1,0:T(8,128)(2,1)}, f32[256,1536]{1,0:T(8,128)}, f32[192,2240]{1,0:T(8,128)}, f32[192,2240]{1,0:T(8,128)}, f32[192,2240]{1,0:T(8,12...) custom-call(bf16[256,1536]{1,0:T(8,128)(2,1)} %get-tuple-element.63., ...), custom_call_target="tpu_custom_call" | custom-call | tf_op jit(solution)/shard_map/results/pallas_call | solution.py:1523
  (2 shorter events, 0.0 us)

commit v2 on v1

--- a/solution.py
+++ b/solution.py
@@ -230,9 +230,9 @@
 
 def front_kernel(
     seq_size,
-    tok_ref, cot_ref, pack_ref, wq_ref, wk_ref, wv_ref, wo_ref, cos_ref, sin_ref, seg_ref, wg_ref, wu_ref, wd_ref,
-    wqg_ref, wog_ref, wkvg_ref, x2g_ref, cotg_ref, hidden_ref, n1_ref, q_ref, kv_ref, p_ref, ctx_ref, act_ref, gg_ref, gu_ref,
-    packs, kv_v, ctx_v, hidden_v, x2_v, cot_v, wo_v, wog_v, wqg_v, p_sems, send, recv, local,
+    tok_ref, cot_ref, gain_one_ref, gain_two_ref, qb_ref, kb_ref, vb_ref, wq_ref, wk_ref, wv_ref, wo_ref, cos_ref, sin_ref, seg_ref, wg_ref, wu_ref, wd_ref,
+    wqg_ref, wog_ref, wkvg_ref, x2g_ref, cotg_ref, hidden_ref, n1_ref, q_ref, kv_ref, p_ref, ctx_ref, act_ref, gg_ref, gu_ref, pack_out_ref,
+    pack_ref, packs, kv_v, ctx_v, hidden_v, x2_v, cot_v, wo_v, wog_v, wqg_v, p_sems, send, recv, local,
 ):
     place = Place(seq_size)
     wires = Wires(send, recv, local)
@@ -246,6 +246,12 @@
     ff = wg_ref.shape[0]
 
     kv_v[...] = jnp.zeros_like(kv_v)
+    pack_ref[...] = jnp.zeros_like(pack_ref)
+    for row, start, vector in (
+        (0, 0, gain_one_ref), (1, 0, gain_two_ref), (2, 0, qb_ref), (2, qw, kb_ref), (2, qw + hd, vb_ref)
+    ):
+        count = vector.shape[0]
+        pack_ref[row, start : start + count] = vector[...].astype(f32)
     barrier = greet(
         [place.across_x, place.across_y, place.diagonal, place.sibling],
         [(place.has_below, place.below), (place.has_above, place.above)],
@@ -299,6 +305,8 @@
     save_two = wires.copy(x2_v, x2g_ref)
     save_cot = wires.copy(cot_v, cotg_ref)
     load_cot.start()
+    save_pack = wires.copy(pack_ref, pack_out_ref)
+    save_pack.start()
     save_kv = wires.copy(kv_v, kv_ref)
     save_ctx = wires.copy(ctx_v, ctx_ref)
     save_hidden = wires.copy(hidden_v, hidden_ref)
@@ -530,7 +538,7 @@
         pltpu.VMEM((2, 3, tok, ff), bf16),
     )
 
-    for copy in [save_kv, save_ctx, save_hidden, save_wq, save_wo, save_two, save_cot]:
+    for copy in [save_pack, save_kv, save_ctx, save_hidden, save_wq, save_wo, save_two, save_cot]:
         copy.wait()
     for copy in kvx + [kvs] + packed:
         copy.wait_send()
@@ -548,7 +556,7 @@
                     ups[j].wait_send()
 
 
-def front(seq_size, tok, cot, pack, wq, wk, wv, wo, cosine, sine, segs, wg, wu, wd):
+def front(seq_size, tok, cot, gain_one, gain_two, qb, kb, vb, wq, wk, wv, wo, cosine, sine, segs, wg, wu, wd):
     tokens, width = tok.shape
     span = tokens // 2
     qw, hd = wq.shape[1], cosine.shape[1]
@@ -572,10 +580,12 @@
         shape((4 * tokens, ff), bf16),
         shape((4 * tokens, ff), bf16),
         shape((4 * tokens, ff), bf16),
+        shape((8, width), f32),
     )
     remotes = 6 + 8 + 15 + 2 * chips + 8
     scratch = [
-        pltpu.VMEM((3,) + pack.shape, f32),
+        pltpu.VMEM((8, width), f32),
+        pltpu.VMEM((3, 8, width), f32),
         pltpu.VMEM((4, 2, keys, hd), bf16),
         pltpu.VMEM((4, tokens, qw), bf16),
         pltpu.VMEM((tokens, width), f32),
@@ -592,14 +602,14 @@
     return pl.pallas_call(
         functools.partial(front_kernel, seq_size),
         out_shape=outs,
-        in_specs=[VMEM, ANY, VMEM, ANY, ANY, ANY, ANY, VMEM, VMEM, VMEM, ANY, ANY, ANY],
+        in_specs=[VMEM, ANY, VMEM, VMEM, VMEM, VMEM, VMEM, ANY, ANY, ANY, ANY, VMEM, VMEM, VMEM, ANY, ANY, ANY],
         out_specs=tuple([ANY] * len(outs)),
         scratch_shapes=scratch,
         name="attention_front",
         compiler_params=pltpu.CompilerParams(
             collective_id=0, has_side_effects=True, vmem_limit_bytes=62 * 2**20
         ),
-    )(tok, cot, pack, wq, wk, wv, wo, cosine, sine, segs, wg, wu, wd)
+    )(tok, cot, gain_one, gain_two, qb, kb, vb, wq, wk, wv, wo, cosine, sine, segs, wg, wu, wd)
 
 
 def add_rows(total, extra, step=32):
@@ -1128,20 +1138,8 @@
             room = r.kv_room
             line_kv = LineSumDown(place, wires, lambda d: dkv.at[d, c], r.kv_land, room.at[0])
             share_kv.start()
-            for b in range(4):
-                for row in range(2):
-                    here = pl.ds(row * span, span)
-                    for n in range(heads):
-                        part = dq[b, row, n * span : (n + 1) * span, :] * scaling
-                        part = turn(part, cosine[here, :], -sine[here, :])
-                        rhs[b, here, n * hd : (n + 1) * hd] = part.astype(bf16)
-            for name in ("wq0", "wq1", "wk", "wv", "wkv1", "n1"):
-                loads[name].wait()
-
             def query_part(fullq):
                 shares, finish = add_cores(fullq, r.core_land, q_parts)
-                for b in range(4):
-                    fullq[b] = dot(n1[...], rhs[b], ((0,), (0,))).astype(bf16).reshape(chips, 2, rb, qw)
                 share_kv.wait_recv()
                 for i in range(0, chips, 2):
                     wires.fetch([r.kv_core.at[i], r.kv_core.at[i + 1]], [room.at[0], room.at[1]])
@@ -1151,9 +1149,18 @@
                     line_kv.send(w)
                 for w in range(1, last):
                     lines[1].send(w)
-                lines[2].send(0)
-                for copy in shares:
-                    copy.start()
+                for b in range(4):
+                    for row in range(2):
+                        here = pl.ds(row * span, span)
+                        for n in range(heads):
+                            part = dq[b, row, n * span : (n + 1) * span, :] * scaling
+                            part = turn(part, cosine[here, :], -sine[here, :])
+                            rhs[b, here, n * hd : (n + 1) * hd] = part.astype(bf16)
+                for name in ("wq0", "wq1", "wk", "wv", "wkv1", "n1"):
+                    loads[name].wait()
+                for b in range(4):
+                    fullq[b] = dot(n1[...], rhs[b], ((0,), (0,))).astype(bf16).reshape(chips, 2, rb, qw)
+                    shares[b].start()
                 grad_one[...] = dot(rhs[0], wq[0], ((1,), (1,)))
                 if last > 1:
                     line_kv.forward(1)
@@ -1241,8 +1248,9 @@
                 plane.end()
                 for i in range(chips):
                     totals[i] = plane.value(pl.ds(i * rb, rb)).astype(bf16)
-            for spread in spread_sums:
-                spread.send()
+                if plane is plane_w:
+                    spread_w.send()
+                    lines[2].send(0)
             for w in range(2, last):
                 lines[1].forward(w)
             plane_out.end()
@@ -1278,6 +1286,8 @@
             spread_smalls = Spread(place, wires, lambda d: small, lambda d: smalls.at[d])
             spread_pieces.send()
             spread_smalls.send()
+            spread_o.send()
+            spread_q.send()
             for w in range(1, last):
                 lines[2].send(w)
             lines[1].finish()
@@ -1552,12 +1562,9 @@
     sine = jnp.sin(phase) * jnp.where(jnp.arange(hd) < hd // 2, -1.0, 1.0)
     tok = tokens.reshape(count, width)
     cot = cotangent.reshape(count, width)
-    bias = jnp.concatenate([query_bias, key_offset_bias, value_offset_bias])
-    bias = jnp.pad(bias, (0, width - bias.shape[0]))
-    pack = jnp.pad(jnp.stack([attn_gain, mlp_gain, bias]).astype(f32), ((0, 5), (0, 0)))
     gate_rows, up_rows = gate_weight.T, up_weight.T
-    wqg, wog, wkvg, x2g, cotg, hidden, n1, qrot, kv, probs, ctx, act, gg, gu = front(
-        seq_size, tok, cot, pack, query_weight, key_matrix, value_matrix, out_weight, cosine, sine, segment_ids,
+    wqg, wog, wkvg, x2g, cotg, hidden, n1, qrot, kv, probs, ctx, act, gg, gu, pack = front(
+        seq_size, tok, cot, attn_gain, mlp_gain, query_bias, key_offset_bias, value_offset_bias, query_weight, key_matrix, value_matrix, out_weight, cosine, sine, segment_ids,
         gate_rows, up_rows, down_weight,
     )
     made = back(

time: 372 us -> 371 us (level)
  no operation moved by 1% of the time
where the time goes in v2:
time: 371 us; the launch traced here: 367 us
  Pallas kernels  364 us (98%)
    pallas_call x1, Pallas kernels, back(): pl.pallas_call(functools.partial(back_kernel, seq_size, names), out_shape...  246 us
    pallas_call x1, Pallas kernels, front(): pl.pallas_call(functools.partial(front_kernel, seq_size), out_shape=outs,...  109 us
    pallas_call x1, Pallas kernels, last(): pl.pallas_call(functools.partial(last_kernel, list(ins) + list(outs) + li...  8.2 us

profile of v2, /device:TPU:0, one launch (start us, length us, event | category | flops | bytes accessed | tf_op | source)
XLA Modules:
  0.0 366.7 jit_solution(17851520679633541748)
XLA Ops:
  0.7 0.7 convert_bitcast_fusion
  1.4 0.1 compare_select_fusion
  1.4 1.2 fusion
  2.7 109.3 %attention_front.1 = (bf16[3,1536,384]{2,1,0:T(8,128)(2,1)}, bf16[3,384,1536]{2,1,0:T(8,128)(2,1)}, bf16[1536,256]{1,0:T(8,128)(2,1)}, bf16[4,256,1536]{2,1,0:T(...) custom-call(bf16[256,1536]{1,0:T(8,128)(2,1)} %bitcast.17, ...), custom_call_target="tpu_custom_call" | custom-call | tf_op jit(solution)/shard_map/attention_front/pallas_call | solution.py:602
  112.0 246.0 %weight_gradients_and_attention_back.1 = (bf16[256,1536]{1,0:T(8,128)(2,1)}, f32[256,1536]{1,0:T(8,128)}, bf16[3,192,2240]{2,1,0:T(8,128)(2,1)}, bf16[192,384]{1...) custom-call(bf16[1024,1536]{1,0:T(8,128)(2,1)} %bitcast.21, ...), custom_call_target="tpu_custom_call" | custom-call | tf_op jit(solution)/shard_map/weight_gradients_and_attention_back/pallas_call | solution.py:1433
  358.0 8.2 %results.1 = (bf16[256,1536]{1,0:T(8,128)(2,1)}, f32[256,1536]{1,0:T(8,128)}, f32[192,2240]{1,0:T(8,128)}, f32[192,2240]{1,0:T(8,128)}, f32[192,2240]{1,0:T(8,12...) custom-call(bf16[256,1536]{1,0:T(8,128)(2,1)} %get-tuple-element.65., ...), custom_call_target="tpu_custom_call" | custom-call | tf_op jit(solution)/shard_map/results/pallas_call | solution.py:1533
  (1 shorter events, 0.0 us)
